TPU v7x, 128 devices: a whole 4x4x4 slice. The times are simulated.
128 devices in a mesh: pp: 4 (over y), ep: 32 (over x, z, core).
Axes of the slice: x: 4, y: 4, z: 4, core: 2. Of those that a mesh axis runs over, the one named last changes fastest.
Arguments:
- tokens_a: bfloat16 [2048, 7168], P('ep'), may hold values from -51 to 51
- tokens_b: bfloat16 [2048, 7168], P('ep'), may hold values from -51 to 51
- routes_a: int32 [4, 2048, 2], P('pp', 'ep'), may hold values from 0 to 15, all different within a row; in each aligned block of 64 rows (0 to 63, 64 to 127, ..., all dimensions but the last counted through in order) at most 10 rows name the same one
- routes_b: int32 [4, 2048, 2], P('pp', 'ep'), may hold values from 0 to 15, all different within a row; in each aligned block of 64 rows (0 to 63, 64 to 127, ..., all dimensions but the last counted through in order) at most 10 rows name the same one
- affinity_a: float32 [4, 2048, 2], P('pp', 'ep'), may hold values from 0.2 to 1
- affinity_b: float32 [4, 2048, 2], P('pp', 'ep'), may hold values from 0.2 to 1
- gate_w: bfloat16 [4, 7168, 16384], P('pp', None, 'ep'), may hold values from -0.0625 to 0.0625
- up_w: bfloat16 [4, 7168, 16384], P('pp', None, 'ep'), may hold values from -0.0625 to 0.0625
- down_w: bfloat16 [4, 16384, 7168], P('pp', 'ep'), may hold values from -0.1875 to 0.1875
Outputs:
- states_a: bfloat16 [4, 2048, 7168], P('pp', 'ep')
- states_b: bfloat16 [4, 2048, 7168], P('pp', 'ep')
Inputs may be any that keep to these rules, and one draw needn't show every extreme that they name: `routes_a`: in every aligned block of 64 rows of one layer no expert is named more than 10 times, and the 2 experts of a token differ. `routes_b`: as routes_a.
All inputs are finite; a program needn't handle non-finite values.
Results may differ from a plain program's by a relative error of at most 0.013.
Values may be sent and summed in bfloat16 or wider, within the bound.
No kernel may reach another device: no remote copies, remote signals or barrier semaphores. Data moves between devices by JAX's collectives and lax.ppermute only.
A program may use at most 128 MiB of HBM per device.

v0:
```python
import jax
import jax.numpy as jnp
from jax import lax
from jax.sharding import PartitionSpec as P


def from_behind(block, axis, distance):
    devices = range(lax.axis_size(axis))
    route = [(i - distance, i) for i in devices if i - distance in devices]
    return lax.ppermute(block, axis, route)


def normalize(activations):
    values = activations.astype(jnp.float32)
    scale = lax.rsqrt(jnp.mean(values * values, axis=-1, keepdims=True) + 1e-06)
    return (values * scale).astype(jnp.bfloat16)


def slot_index(routes, experts, capacity):
    flattened = routes.reshape(-1)
    onehot = (flattened[:, None] == jnp.arange(experts, dtype=jnp.int32)[None, :]).astype(jnp.int32)
    before = jnp.cumsum(onehot, axis=0) - onehot
    position = jnp.sum(before * onehot, axis=1)
    return flattened * capacity + position


def make_finish(gate_local, up_local, down_local):

    def finish(received):
        source_count, slot_count, feature_width = received.shape
        row_matrix = received.reshape(source_count * slot_count, feature_width)
        gate_act = jnp.dot(row_matrix, gate_local, preferred_element_type=jnp.float32)
        up_act = jnp.dot(row_matrix, up_local, preferred_element_type=jnp.float32)
        hidden = (jax.nn.silu(gate_act) * up_act).astype(jnp.bfloat16)
        partial_rows = jnp.dot(hidden, down_local, preferred_element_type=jnp.float32).astype(
            jnp.bfloat16
        )
        partial_rows = partial_rows.reshape(source_count, slot_count, feature_width)
        return lax.all_to_all(partial_rows, "ep", split_axis=0, concat_axis=0, tiled=True)

    return finish


def moe_layer(activations, routes, affinity, finish, experts, capacity):
    token_count, feature_width = activations.shape
    route_count = routes.shape[1]
    normed = normalize(activations)
    target = slot_index(routes, experts, capacity)
    select = (jnp.arange(experts * capacity, dtype=jnp.int32)[:, None] == target[None, :]).astype(
        jnp.bfloat16
    )
    repeated = jnp.repeat(normed, route_count, axis=0)
    buffer = jnp.dot(select, repeated, preferred_element_type=jnp.float32).astype(jnp.bfloat16)
    outgoing = jnp.repeat(buffer.reshape(experts, capacity, feature_width), 2, axis=0)
    returned = finish(lax.all_to_all(outgoing, "ep", split_axis=0, concat_axis=0, tiled=True))
    paired = returned.reshape(experts, 2, capacity, feature_width).astype(jnp.float32)
    combined = (paired[:, 0] + paired[:, 1]).astype(jnp.bfloat16).astype(jnp.float32)
    combined = combined.reshape(experts * capacity, feature_width)
    picked = jnp.take(combined, target, axis=0).reshape(token_count, route_count, feature_width)
    updated = activations.astype(jnp.float32) + jnp.sum(affinity[:, :, None] * picked, axis=1)
    return updated.astype(jnp.bfloat16)


def shards(tokens_a, tokens_b, routes_a, routes_b, affinity_a, affinity_b, gate_w, up_w, down_w):
    section_count = lax.axis_size("pp")
    experts = lax.axis_size("ep") // 2
    token_count = tokens_a.shape[0]
    route_count = routes_a.shape[2]
    capacity = 2 * (token_count * route_count // lax.axis_size("ep")) + 2
    section_number = lax.axis_index("pp")
    finish = make_finish(gate_w[0], up_w[0], down_w[0])
    forward_input = tokens_a
    reverse_input = tokens_b
    forward_state = jnp.zeros_like(tokens_a)
    reverse_state = jnp.zeros_like(tokens_b)
    for moment in range(section_count):
        forward_turn = section_number == moment
        reverse_turn = section_number == section_count - 1 - moment
        layer_input = jnp.where(forward_turn, forward_input, reverse_input)
        layer_routes = jnp.where(forward_turn, routes_a[0], routes_b[0])
        layer_affinity = jnp.where(forward_turn, affinity_a[0], affinity_b[0])
        result = moe_layer(layer_input, layer_routes, layer_affinity, finish, experts, capacity)
        forward_state = jnp.where(forward_turn, result, forward_state)
        reverse_state = jnp.where(reverse_turn, result, reverse_state)
        if moment + 1 < section_count:
            forward_input = from_behind(result, "pp", 1)
            reverse_input = from_behind(result, "pp", -1)
    return (forward_state[None], reverse_state[None])


def solution(mesh):
    placed = (
        P("ep", None),
        P("ep", None),
        P("pp", "ep", None),
        P("pp", "ep", None),
        P("pp", "ep", None),
        P("pp", "ep", None),
        P("pp", None, "ep"),
        P("pp", None, "ep"),
        P("pp", "ep", None),
    )
    return jax.shard_map(
        shards,
        mesh=mesh,
        in_specs=placed,
        out_specs=(P("pp", "ep", None), P("pp", "ep", None)),
        check_vma=False,
    )
```

profile of v0, /device:TPU:0, one launch (start us, length us, event | category | flops | bytes accessed | tf_op | source)
XLA Modules:
  0.0 1289.0 jit_solution(8854819472173972417)
XLA Ops:
  15.0 92.4 %all_to_all.40 = bf16[32,10,7168]{2,1,0:T(8,128)(2,1)} all-to-all(bf16[32,10,7168]{2,1,0:T(8,128)(2,1)S(1)} %bitcast.151), channel_id=1, replica_groups=mesh['pp'=4,'ep'=32] {'ep'}, dimensions={0} | all-to-all | bytes 9175040 | tf_op jit(solution)/shard_map/all_to_all | solution.py:55
  107.4 8.1 reshape.308
  115.5 7.0 fusion.26
  122.5 13.6 %convolution_convert_fusion.3 = bf16[320,7168]{1,0:T(8,128)(2,1)} fusion(bf16[1,512,7168]{2,1,0:T(8,128)(2,1)} %param.19, bf16[320,7168]{1,0:T(8,128)(2,1)} %reshape.308, bf16[1,7168,512]{2,1,0:T(8,128)(2,1)} %param.18, f32[320,512]{1,0:T(8,128)S(1)} %fusion.26), kind=kOutput, calls=%fused_computation.7 | convolution fusion | flops 4700897280 | bytes 24510464 | tf_op jit(solution)/shard_map/dot_general | solution.py:35
  136.0 7.8 reshape.309
  143.8 5.2 all-to-all-start.1
  149.8 97.4 %all-to-all-done.1 = bf16[32,10,7168]{2,1,0:T(8,128)(2,1)} async-done(((bf16[32,10,7168]{2,1,0:T(8,128)(2,1)}), bf16[32,10,7168]{2,1,0:T(8,128)(2,1)}, u32[]{:S(2)}, u32[]{:S(2)}) %all-to-all-start.1) | async-done | bytes 4587552 | tf_op jit(solution)/shard_map/all_to_all | solution.py:39
  247.2 10.2 convert.8
  257.4 9.2 fusion.28
  266.7 5.7 reshape.330
  272.4 7.3 gather_fusion
  279.7 4.2 broadcast_select_fusion.3
  284.0 5.5 reshape.310
  289.5 7.1 multiply_reduce_fusion.3
  296.8 3.5 collective-permute-start
  302.6 10.7 collective-permute-done
  313.3 4.3 collective-permute-done.1
  329.9 107.7 %all_to_all.41 = bf16[32,10,7168]{2,1,0:T(8,128)(2,1)} all-to-all(bf16[32,10,7168]{2,1,0:T(8,128)(2,1)S(1)} %bitcast.152), channel_id=1, replica_groups=mesh['pp'=4,'ep'=32] {'ep'}, dimensions={0} | all-to-all | bytes 9175040 | tf_op jit(solution)/shard_map/all_to_all | solution.py:55
  437.5 8.1 reshape.314
  445.6 7.0 fusion.24
  452.6 13.6 %convolution_convert_fusion.2 = bf16[320,7168]{1,0:T(8,128)(2,1)} fusion(bf16[1,512,7168]{2,1,0:T(8,128)(2,1)} %param.19, bf16[320,7168]{1,0:T(8,128)(2,1)} %reshape.314, bf16[1,7168,512]{2,1,0:T(8,128)(2,1)} %param.18, f32[320,512]{1,0:T(8,128)S(1)} %fusion.24), kind=kOutput, calls=%fused_computation.6 | convolution fusion | flops 4700897280 | bytes 24510464 | tf_op jit(solution)/shard_map/dot_general | solution.py:35
  466.2 7.8 reshape.315
  474.0 5.3 all-to-all-start.3
  479.5 98.0 %all-to-all-done.3 = bf16[32,10,7168]{2,1,0:T(8,128)(2,1)} async-done(((bf16[32,10,7168]{2,1,0:T(8,128)(2,1)}), bf16[32,10,7168]{2,1,0:T(8,128)(2,1)}, u32[]{:S(2)}, u32[]{:S(2)}) %all-to-all-start.3) | async-done | bytes 4587552 | tf_op jit(solution)/shard_map/all_to_all | solution.py:39
  577.5 10.2 convert.9
  587.7 9.2 fusion.29
  596.9 5.7 reshape.332
  602.7 7.3 gather_fusion.1
  610.0 4.2 broadcast_select_fusion.2
  614.2 5.5 reshape.316
  619.7 7.1 multiply_reduce_fusion.2
  631.6 10.7 collective-permute-done.2
  642.3 4.9 collective-permute-done.3
  659.6 107.7 %all_to_all.42 = bf16[32,10,7168]{2,1,0:T(8,128)(2,1)} all-to-all(bf16[32,10,7168]{2,1,0:T(8,128)(2,1)S(1)} %bitcast.153), channel_id=1, replica_groups=mesh['pp'=4,'ep'=32] {'ep'}, dimensions={0} | all-to-all | bytes 9175040 | tf_op jit(solution)/shard_map/all_to_all | solution.py:55
  767.3 8.1 reshape.320
  775.4 7.0 fusion.22
  782.4 13.6 %convolution_convert_fusion.1 = bf16[320,7168]{1,0:T(8,128)(2,1)} fusion(bf16[1,512,7168]{2,1,0:T(8,128)(2,1)} %param.19, bf16[320,7168]{1,0:T(8,128)(2,1)} %reshape.320, bf16[1,7168,512]{2,1,0:T(8,128)(2,1)} %param.18, f32[320,512]{1,0:T(8,128)S(1)} %fusion.22), kind=kOutput, calls=%fused_computation.5 | convolution fusion | flops 4700897280 | bytes 24510464 | tf_op jit(solution)/shard_map/dot_general | solution.py:35
  795.9 7.8 reshape.321
  803.7 5.3 all-to-all-start.5
  809.1 98.0 %all-to-all-done.5 = bf16[32,10,7168]{2,1,0:T(8,128)(2,1)} async-done(((bf16[32,10,7168]{2,1,0:T(8,128)(2,1)}), bf16[32,10,7168]{2,1,0:T(8,128)(2,1)}, u32[]{:S(2)}, u32[]{:S(2)}) %all-to-all-start.5) | async-done | bytes 4587552 | tf_op jit(solution)/shard_map/all_to_all | solution.py:39
  907.1 10.2 convert.10
  917.4 9.2 fusion.30
  926.6 5.7 reshape.334
  932.4 7.3 gather_fusion.2
  939.7 4.2 broadcast_select_fusion.1
  943.9 5.5 reshape.322
  949.4 7.1 multiply_reduce_fusion.1
  956.8 3.7 collective-permute-start.4
  962.9 10.5 collective-permute-done.4
  973.4 4.3 collective-permute-done.5
  990.0 107.7 %all_to_all.43 = bf16[32,10,7168]{2,1,0:T(8,128)(2,1)} all-to-all(bf16[32,10,7168]{2,1,0:T(8,128)(2,1)S(1)} %bitcast.154), channel_id=1, replica_groups=mesh['pp'=4,'ep'=32] {'ep'}, dimensions={0} | all-to-all | bytes 9175040 | tf_op jit(solution)/shard_map/all_to_all | solution.py:55
  1097.7 8.1 reshape.326
  1105.7 7.0 fusion.20
  1112.7 13.6 %convolution_convert_fusion = bf16[320,7168]{1,0:T(8,128)(2,1)} fusion(bf16[1,512,7168]{2,1,0:T(8,128)(2,1)} %param.19, bf16[320,7168]{1,0:T(8,128)(2,1)} %reshape.326, bf16[1,7168,512]{2,1,0:T(8,128)(2,1)} %param.18, f32[320,512]{1,0:T(8,128)S(1)} %fusion.20), kind=kOutput, calls=%fused_computation.4 | convolution fusion | flops 4700897280 | bytes 24510464 | tf_op jit(solution)/shard_map/dot_general | solution.py:35
  1126.3 7.8 reshape.327
  1134.1 5.2 all-to-all-start.7
  1139.5 98.0 %all-to-all-done.7 = bf16[32,10,7168]{2,1,0:T(8,128)(2,1)} async-done(((bf16[32,10,7168]{2,1,0:T(8,128)(2,1)}), bf16[32,10,7168]{2,1,0:T(8,128)(2,1)}, u32[]{:S(2)}, u32[]{:S(2)}) %all-to-all-start.7) | async-done | bytes 4587552 | tf_op jit(solution)/shard_map/all_to_all | solution.py:39
  1237.5 10.2 convert.11
  1247.7 9.2 fusion.31
  1257.0 5.7 reshape.336
  1262.7 7.3 gather_fusion.3
  1270.0 4.2 broadcast_select_fusion
  1274.2 5.5 reshape.328
  1279.8 7.3 multiply_reduce_fusion
  (102 shorter events, 63.6 us)
Async XLA Ops:
  143.8 5.2 copy-start.10
  143.8 5.3 copy-start.11
  143.8 103.4 %all-to-all-start.1 = ((bf16[32,10,7168]{2,1,0:T(8,128)(2,1)}), bf16[32,10,7168]{2,1,0:T(8,128)(2,1)}, u32[]{:S(2)}, u32[]{:S(2)}) async-start(bf16[32,10,7168]{2,1,0:T(8,128)(2,1)} %reshape.309), calls=%async_computation.1 | async-start | bytes 14680064 | tf_op jit(solution)/shard_map/all_to_all | solution.py:39
  296.8 22.3 %copy-start = (bf16[64,7168]{1,0:T(8,128)(2,1)}, bf16[64,7168]{1,0:T(8,128)(2,1)S(1)}, u32[]{:S(2)}) copy-start(bf16[64,7168]{1,0:T(8,128)(2,1)S(1)} %fusion.34) | copy-start | bytes 2752516
  296.8 16.4 %collective-permute-start = (bf16[64,7168]{1,0:T(8,128)(2,1)S(1)}, bf16[64,7168]{1,0:T(8,128)(2,1)S(1)}, u32[]{:S(2)}, u32[]{:S(2)}) collective-permute-start(bf16[64,7168]{1,0:T(8,128)(2,1)S(1)} %fusion.34), channel_id=1, source_target_pairs={{0,32},{32,64},{64,96},{1,33},{33,65},{65,97},{2,34},{34,66},{66,9... | collective-permute-start | bytes 2752520 | tf_op jit(solution)/shard_map/ppermute | solution.py:10
  300.4 17.1 %collective-permute-start.1 = (bf16[64,7168]{1,0:T(8,128)(2,1)S(1)}, bf16[64,7168]{1,0:T(8,128)(2,1)}, u32[]{:S(2)}, u32[]{:S(2)}) collective-permute-start(bf16[64,7168]{1,0:T(8,128)(2,1)S(1)} %fusion.34), channel_id=1, source_target_pairs={{32,0},{64,32},{96,64},{33,1},{65,33},{97,65},{34,2},{66,34},{98,6... | collective-permute-start | bytes 2752520 | tf_op jit(solution)/shard_map/ppermute | solution.py:10
  474.0 103.5 %all-to-all-start.3 = ((bf16[32,10,7168]{2,1,0:T(8,128)(2,1)}), bf16[32,10,7168]{2,1,0:T(8,128)(2,1)}, u32[]{:S(2)}, u32[]{:S(2)}) async-start(bf16[32,10,7168]{2,1,0:T(8,128)(2,1)} %reshape.315), calls=%async_computation.3 | async-start | bytes 14680064 | tf_op jit(solution)/shard_map/all_to_all | solution.py:39
  619.7 11.2 copy-start.9
  627.1 21.8 %copy-start.2 = (bf16[64,7168]{1,0:T(8,128)(2,1)}, bf16[64,7168]{1,0:T(8,128)(2,1)S(1)}, u32[]{:S(2)}) copy-start(bf16[64,7168]{1,0:T(8,128)(2,1)S(1)} %fusion.37) | copy-start | bytes 2752516
  627.1 15.2 %collective-permute-start.2 = (bf16[64,7168]{1,0:T(8,128)(2,1)S(1)}, bf16[64,7168]{1,0:T(8,128)(2,1)S(1)}, u32[]{:S(2)}, u32[]{:S(2)}) collective-permute-start(bf16[64,7168]{1,0:T(8,128)(2,1)S(1)} %fusion.37), channel_id=1, source_target_pairs={{0,32},{32,64},{64,96},{1,33},{33,65},{65,97},{2,34},{34,66},{66,9... | collective-permute-start | bytes 2752520 | tf_op jit(solution)/shard_map/ppermute | solution.py:10
  629.4 17.8 %collective-permute-start.3 = (bf16[64,7168]{1,0:T(8,128)(2,1)S(1)}, bf16[64,7168]{1,0:T(8,128)(2,1)}, u32[]{:S(2)}, u32[]{:S(2)}) collective-permute-start(bf16[64,7168]{1,0:T(8,128)(2,1)S(1)} %fusion.37), channel_id=1, source_target_pairs={{32,0},{64,32},{96,64},{33,1},{65,33},{97,65},{34,2},{66,34},{98,6... | collective-permute-start | bytes 2752520 | tf_op jit(solution)/shard_map/ppermute | solution.py:10
  803.7 5.3 copy-start.8
  803.7 103.4 %all-to-all-start.5 = ((bf16[32,10,7168]{2,1,0:T(8,128)(2,1)}), bf16[32,10,7168]{2,1,0:T(8,128)(2,1)}, u32[]{:S(2)}, u32[]{:S(2)}) async-start(bf16[32,10,7168]{2,1,0:T(8,128)(2,1)} %reshape.321), calls=%async_computation.5 | async-start | bytes 14680064 | tf_op jit(solution)/shard_map/all_to_all | solution.py:39
  949.4 12.8 copy-start.7
  956.8 22.5 %copy-start.4 = (bf16[64,7168]{1,0:T(8,128)(2,1)}, bf16[64,7168]{1,0:T(8,128)(2,1)S(1)}, u32[]{:S(2)}) copy-start(bf16[64,7168]{1,0:T(8,128)(2,1)S(1)} %fusion.40) | copy-start | bytes 2752516
  956.8 16.6 %collective-permute-start.4 = (bf16[64,7168]{1,0:T(8,128)(2,1)S(1)}, bf16[64,7168]{1,0:T(8,128)(2,1)S(1)}, u32[]{:S(2)}, u32[]{:S(2)}) collective-permute-start(bf16[64,7168]{1,0:T(8,128)(2,1)S(1)} %fusion.40), channel_id=1, source_target_pairs={{0,32},{32,64},{64,96},{1,33},{33,65},{65,97},{2,34},{34,66},{66,9... | collective-permute-start | bytes 2752520 | tf_op jit(solution)/shard_map/ppermute | solution.py:10
  960.5 17.1 %collective-permute-start.5 = (bf16[64,7168]{1,0:T(8,128)(2,1)S(1)}, bf16[64,7168]{1,0:T(8,128)(2,1)}, u32[]{:S(2)}, u32[]{:S(2)}) collective-permute-start(bf16[64,7168]{1,0:T(8,128)(2,1)S(1)} %fusion.40), channel_id=1, source_target_pairs={{32,0},{64,32},{96,64},{33,1},{65,33},{97,65},{34,2},{66,34},{98,6... | collective-permute-start | bytes 2752520 | tf_op jit(solution)/shard_map/ppermute | solution.py:10
  1134.1 5.2 copy-start.6
  1134.1 103.4 %all-to-all-start.7 = ((bf16[32,10,7168]{2,1,0:T(8,128)(2,1)}), bf16[32,10,7168]{2,1,0:T(8,128)(2,1)}, u32[]{:S(2)}, u32[]{:S(2)}) async-start(bf16[32,10,7168]{2,1,0:T(8,128)(2,1)} %reshape.327), calls=%async_computation.7 | async-start | bytes 14680064 | tf_op jit(solution)/shard_map/all_to_all | solution.py:39
  1279.8 7.3 copy-start.1
  1279.8 7.3 copy-start.3
  1279.8 7.3 copy-start.5
where the time goes:
time: 1310 us; the launch traced here: 1290 us
  waiting for transfers between devices  437 us (33%)
  blocking collectives  415 us (32%)
  local copies, waits for them, and re-layouts  172 us (13%)
  other arithmetic  137 us (10%)
  matrix products  91.2 us (7%)
  starting transfers between devices  35.3 us (3%)
    all_to_all x4, blocking collectives, moe_layer(): lax.all_to_all(outgoing, 'ep', split_axis=0, concat_axis=0, tiled=True)  415 us
    all_to_all x4, waiting for transfers between devices, finish(): lax.all_to_all(partial_rows, 'ep', split_axis=0, concat_axis=0, tiled=True)  391 us
    dot_general x4, matrix products, finish(): jnp.dot(hidden, down_local, preferred_element_type=jnp.float32)  54.3 us
    ppermute x6, waiting for transfers between devices, from_behind(): return lax.ppermute(block, axis, route)  45.3 us
    convert_element_type x4, other arithmetic, moe_layer(): returned.reshape(experts, 2, capacity, feature_width).astype(jnp.float32)  40.9 us
    convert_element_type x4, other arithmetic, moe_layer(): (paired[:, 0] + paired[:, 1]).astype(jnp.bfloat16).astype(jnp.float32)  36.9 us
    reshape x4, local copies, waits for them, and re-layouts, finish(): row_matrix = received.reshape(source_count * slot_count, feature_width)  32.4 us
    reshape x4, local copies, waits for them, and re-layouts, finish(): partial_rows = partial_rows.reshape(source_count, slot_count, feature_width)  31.3 us
  transfers between devices with their start and end apart: 10, of which 10 were waited for; matrix products, arithmetic and copies ran while one was open for 0% of the time, Pallas kernels for 0%

commit v1 on v0

v1 whole, which is shorter than its diff:
```python
import functools

import jax
import jax.numpy as jnp
import numpy as np
from jax import lax
from jax.experimental import pallas as pl
from jax.experimental.pallas import tpu as pltpu
from jax.sharding import PartitionSpec as P

MIB = 1 << 20
PIECES = 4
GROUP = 8


def vmem():
    return pl.BlockSpec(memory_space=pltpu.VMEM)


def params(mib):
    return pltpu.CompilerParams(vmem_limit_bytes=mib * MIB)


def row_codes(experts, capacity):
    expert, piece, slot = np.meshgrid(
        np.arange(experts), np.arange(PIECES), np.arange(capacity), indexing="ij"
    )
    return (piece * experts * capacity + expert * capacity + slot).reshape(-1).astype(np.int32)


def group_permutation(capacity):
    rows = GROUP * PIECES * capacity
    result = np.zeros((rows, rows), np.float32)
    for piece in range(PIECES):
        for chip in range(GROUP):
            for slot in range(capacity):
                to = (piece * GROUP + chip) * capacity + slot
                result[to, (chip * PIECES + piece) * capacity + slot] = 1
    return result


def dispatch_kernel(x_ref, code_ref, row_ref, out_ref, stacked):
    tokens, width = x_ref.shape
    part = width // PIECES
    values = x_ref[...].astype(jnp.float32)
    scale = lax.rsqrt(jnp.mean(values * values, axis=-1, keepdims=True) + 1e-06)
    for piece in range(PIECES):
        columns = slice(piece * part, (piece + 1) * part)
        stacked[piece * tokens : (piece + 1) * tokens, :] = (
            x_ref[:, columns].astype(jnp.float32) * scale
        ).astype(jnp.bfloat16)
    rows = row_ref[...]
    hit = (rows == code_ref[0:1, :]) | (rows == code_ref[1:2, :])
    select = jnp.where(hit, 1.0, 0.0).astype(jnp.bfloat16)
    for start in range(0, part, 256):
        columns = slice(start, start + 256)
        out_ref[:, columns] = jnp.dot(
            select, stacked[:, columns], preferred_element_type=jnp.float32
        ).astype(jnp.bfloat16)


def dispatch(x, code, rows):
    tokens, width = x.shape
    wire, part = rows.shape[0], width // PIECES
    return pl.pallas_call(
        dispatch_kernel,
        out_shape=jax.ShapeDtypeStruct((wire, part), jnp.bfloat16),
        in_specs=[vmem()] * 3,
        out_specs=vmem(),
        scratch_shapes=[pltpu.VMEM((PIECES * tokens, part), jnp.bfloat16)],
        compiler_params=params(24),
        cost_estimate=pl.CostEstimate(
            flops=2 * wire * PIECES * tokens * part, bytes_accessed=4 * MIB, transcendentals=0
        ),
        name="dispatch",
    )(x, code, rows)


def hidden_kernel(wire_ref, perm_ref, gate_ref, up_ref, out_ref, rows, gate_sum, up_sum):
    piece = pl.program_id(0)
    height = perm_ref.shape[0]
    span = wire_ref.shape[0] // (rows.shape[0] // height)
    for group in range(rows.shape[0] // height):
        rows[group * height : (group + 1) * height, :] = jnp.dot(
            perm_ref[...],
            wire_ref[group * span : (group + 1) * span, :],
            preferred_element_type=jnp.float32,
        ).astype(jnp.bfloat16)
    gate = jnp.dot(rows[...], gate_ref[...], preferred_element_type=jnp.float32)
    up = jnp.dot(rows[...], up_ref[...], preferred_element_type=jnp.float32)

    @pl.when(piece == 0)
    def _():
        gate_sum[...] = gate
        up_sum[...] = up

    @pl.when(piece > 0)
    def _():
        gate_sum[...] += gate
        up_sum[...] += up

    @pl.when(piece == PIECES - 1)
    def _():
        out_ref[...] = (jax.nn.silu(gate_sum[...]) * up_sum[...]).astype(jnp.bfloat16)


def hidden_units(wire, perm, gate_w, up_w):
    wire_rows, part = wire.shape
    rows = wire_rows // PIECES
    width, units = gate_w.shape
    height = perm.shape[0] // PIECES
    return pl.pallas_call(
        hidden_kernel,
        out_shape=jax.ShapeDtypeStruct((rows, units), jnp.bfloat16),
        grid=(PIECES,),
        in_specs=[
            pl.BlockSpec((wire_rows, part), lambda p: (0, 0)),
            pl.BlockSpec((height, perm.shape[1]), lambda p: (p, 0)),
            pl.BlockSpec((part, units), lambda p: (p, 0)),
            pl.BlockSpec((part, units), lambda p: (p, 0)),
        ],
        out_specs=pl.BlockSpec((rows, units), lambda p: (0, 0)),
        scratch_shapes=[
            pltpu.VMEM((rows, part), jnp.bfloat16),
            pltpu.VMEM((rows, units), jnp.float32),
            pltpu.VMEM((rows, units), jnp.float32),
        ],
        compiler_params=params(32),
        cost_estimate=pl.CostEstimate(
            flops=4 * rows * width * units, bytes_accessed=16 * MIB, transcendentals=rows * units
        ),
        name="hidden_units",
    )(wire, perm, gate_w, up_w)


def down_kernel(hidden_ref, down_ref, out_ref):
    out_ref[...] = jnp.dot(
        hidden_ref[...], down_ref[...], preferred_element_type=jnp.float32
    ).astype(jnp.bfloat16)


def down_rows(hidden, down_w):
    rows, units = hidden.shape
    width = down_w.shape[1]
    step = width // 4
    return pl.pallas_call(
        down_kernel,
        out_shape=jax.ShapeDtypeStruct((rows, width), jnp.bfloat16),
        grid=(width // step,),
        in_specs=[
            pl.BlockSpec((rows, units), lambda n: (0, 0)),
            pl.BlockSpec((units, step), lambda n: (0, n)),
        ],
        out_specs=pl.BlockSpec((rows, step), lambda n: (0, n)),
        compiler_params=params(24),
        cost_estimate=pl.CostEstimate(
            flops=2 * rows * width * units, bytes_accessed=10 * MIB, transcendentals=0
        ),
        name="down_rows",
    )(hidden, down_w)


def gather_kernel(own_ref, other_ref, perm_ref, out_ref, stacked):
    rows, width = own_ref.shape
    part = width // PIECES
    span = perm_ref.shape[0]
    height = span // PIECES
    for group in range(rows // height):
        lines = slice(group * height, (group + 1) * height)
        for piece in range(PIECES):
            columns = slice(piece * part, (piece + 1) * part)
            stacked[piece * height : (piece + 1) * height, :] = (
                own_ref[lines, columns].astype(jnp.float32)
                + other_ref[lines, columns].astype(jnp.float32)
            ).astype(jnp.bfloat16)
        for start in range(0, part, 256):
            columns = slice(start, start + 256)
            out_ref[group * span : (group + 1) * span, columns] = jnp.dot(
                perm_ref[...], stacked[:, columns], preferred_element_type=jnp.float32
            ).astype(jnp.bfloat16)


def add_halves(own, other, back):
    rows, width = own.shape
    part = width // PIECES
    return pl.pallas_call(
        gather_kernel,
        out_shape=jax.ShapeDtypeStruct((rows * PIECES, part), jnp.bfloat16),
        in_specs=[vmem()] * 3,
        out_specs=vmem(),
        scratch_shapes=[pltpu.VMEM((back.shape[0], part), jnp.bfloat16)],
        compiler_params=params(24),
        cost_estimate=pl.CostEstimate(
            flops=2 * rows * PIECES * back.shape[0] * part, bytes_accessed=7 * MIB, transcendentals=0
        ),
        name="add_halves",
    )(own, other, back)


def combine_kernel(x_ref, wire_ref, code_ref, weight_ref, row_ref, out_ref, factors):
    tokens, width = x_ref.shape
    part = width // PIECES
    count = PIECES * tokens
    rows = row_ref[...]
    table = jnp.where(rows == code_ref[:, 0:1], weight_ref[:, 0:1], 0.0)
    table += jnp.where(rows == code_ref[:, 1:2], weight_ref[:, 1:2], 0.0)
    high = table.astype(jnp.bfloat16)
    factors[:count, :] = high
    factors[count:, :] = (table - high.astype(jnp.float32)).astype(jnp.bfloat16)
    for start in range(0, part, 256):
        both = jnp.dot(
            factors[...], wire_ref[:, start : start + 256], preferred_element_type=jnp.float32
        )
        total = both[:count, :] + both[count:, :]
        for piece in range(PIECES):
            columns = slice(piece * part + start, piece * part + start + 256)
            out_ref[:, columns] = (
                x_ref[:, columns].astype(jnp.float32) + total[piece * tokens : (piece + 1) * tokens]
            ).astype(jnp.bfloat16)


def combine(x, wire, code, weight, rows):
    tokens, width = x.shape
    count = PIECES * tokens
    return pl.pallas_call(
        combine_kernel,
        out_shape=jax.ShapeDtypeStruct((tokens, width), jnp.bfloat16),
        in_specs=[vmem()] * 5,
        out_specs=vmem(),
        scratch_shapes=[pltpu.VMEM((2 * count, wire.shape[0]), jnp.bfloat16)],
        compiler_params=params(24),
        cost_estimate=pl.CostEstimate(
            flops=4 * count * wire.shape[0] * wire.shape[1],
            bytes_accessed=5 * MIB,
            transcendentals=0,
        ),
        name="combine",
    )(x, wire, code, weight, rows)


def slot_codes(routes, experts, capacity):
    flat = routes.reshape(-1)
    order = jnp.arange(flat.shape[0], dtype=jnp.int32)
    earlier = (flat[:, None] == flat[None, :]) & (order[None, :] < order[:, None])
    slot = flat * capacity + jnp.sum(earlier.astype(jnp.int32), axis=1)
    slot = slot.reshape(routes.shape)
    shift = jnp.arange(PIECES, dtype=jnp.int32) * (experts * capacity)
    return (shift[:, None, None] + slot[None]).reshape(-1, routes.shape[1])


def shards(tokens_a, tokens_b, routes_a, routes_b, affinity_a, affinity_b, gate_w, up_w, down_w):
    sections = lax.axis_size("pp")
    devices = lax.axis_size("ep")
    experts = devices // 2
    token_count, width = tokens_a.shape
    capacity = 2 * (token_count * routes_a.shape[2] // devices) + 2
    section = lax.axis_index("pp")
    gate, up, down = gate_w[0], up_w[0], down_w[0]

    codes = row_codes(experts, capacity)
    row_column = jnp.asarray(codes.reshape(-1, 1))
    row_line = jnp.asarray(codes.reshape(1, -1))
    order = group_permutation(capacity)
    to_rows = jnp.asarray(order, jnp.bfloat16)
    to_wire = jnp.asarray(order.T, jnp.bfloat16)

    one_core = [[2 * chip + core for chip in range(experts)] for core in range(2)]
    siblings = [(device, device ^ 1) for device in range(devices)]

    def exchange(wire):
        blocks = wire.reshape(experts, PIECES * capacity, width // PIECES)
        moved = lax.all_to_all(
            blocks, "ep", split_axis=0, concat_axis=0, tiled=True, axis_index_groups=one_core
        )
        return moved.reshape(wire.shape)

    def to_sibling(block):
        return lax.ppermute(block, "ep", siblings)

    codes_a = slot_codes(routes_a[0], experts, capacity)
    codes_b = slot_codes(routes_b[0], experts, capacity)
    weights_a = jnp.tile(affinity_a[0], (PIECES, 1))
    weights_b = jnp.tile(affinity_b[0], (PIECES, 1))

    x = jnp.where(section == 0, tokens_a, tokens_b)
    forward_state = reverse_state = None
    for moment in range(sections):
        last = sections - 1 - moment
        forward_turn = section == moment
        code = jnp.where(forward_turn, codes_a, codes_b)
        weight = jnp.where(forward_turn, weights_a, weights_b)
        own = exchange(dispatch(x, code.T, row_column))
        other = to_sibling(own)
        own_hidden = hidden_units(own, to_rows, gate, up)
        other_hidden = hidden_units(other, to_rows, gate, up)
        other_rows = to_sibling(down_rows(other_hidden, down))
        own_rows = down_rows(own_hidden, down)
        back = exchange(add_halves(own_rows, other_rows, to_wire))
        y = combine(x, back, code, weight, row_line)
        if moment == 0:
            forward_state = reverse_state = y
        else:
            forward_state = jnp.where(forward_turn, y, forward_state)
            reverse_state = jnp.where(section == last, y, reverse_state)
        if moment + 1 < sections:
            x = lax.ppermute(y, "pp", [(moment, moment + 1), (last, last - 1)])
    return (forward_state[None], reverse_state[None])


def solution(mesh):
    placed = (
        P("ep", None),
        P("ep", None),
        P("pp", "ep", None),
        P("pp", "ep", None),
        P("pp", "ep", None),
        P("pp", "ep", None),
        P("pp", None, "ep"),
        P("pp", None, "ep"),
        P("pp", "ep", None),
    )
    return jax.shard_map(
        shards,
        mesh=mesh,
        in_specs=placed,
        out_specs=(P("pp", "ep", None), P("pp", "ep", None)),
        check_vma=False,
    )
```

time: 1310 us -> 526 us (0.40); the launches traced: 1290 us -> 525 us
  blocking collectives: 415 us -> 145 us
  waiting for transfers between devices: 437 us -> 211 us
  other arithmetic: 137 us -> 7.05 us
  local copies, waits for them, and re-layouts: 172 us -> 49.6 us
  matrix products: 91.2 us -> 0 us
  Pallas kernels: 0 us -> 88.7 us
  starting transfers between devices: 35.3 us -> 22.1 us
    all_to_all x4, blocking collectives: 415 us -> 145 us  [exchange(): lax.all_to_all(blocks, 'ep', split_axis=0, concat_axis=0, tiled=True, axi...]
    all_to_all x4, waiting for transfers between devices: 391 us -> 131 us  [exchange(): lax.all_to_all(blocks, 'ep', split_axis=0, concat_axis=0, tiled=True, axi...]
    reshape x20 -> x0, local copies, waits for them, and re-layouts: 103 us -> none  [the longest x4 32.4 us: finish(): row_matrix = received.reshape(source_count * slot_count, feature_width)]
    dot_general x12 -> x0, matrix products: 91.2 us -> none  [the longest x4 54.3 us: finish(): jnp.dot(hidden, down_local, preferred_element_type=jnp.float32)]
    pallas_call x0 -> x28, Pallas kernels: none -> 88.7 us  [the longest x8 43.2 us: hidden_units(): pl.pallas_call(hidden_kernel, out_shape=jax.ShapeDtypeStruct((rows, units...]
    convert_element_type x19 -> x0, other arithmetic: 79.8 us -> none  [the longest x4 40.9 us: moe_layer(): returned.reshape(experts, 2, capacity, feature_width).astype(jnp.float32)]
    unnamed x24 -> x88, local copies, waits for them, and re-layouts: 0.05 us -> 46.9 us
    reduce_sum x12 -> x2, other arithmetic: 35.8 us -> 0.35 us  [slot_codes(): slot = flat * capacity + jnp.sum(earlier.astype(jnp.int32), axis=1)]
  transfers between devices with their start and end apart: 10 -> 15, of which waited for: 10 -> 10; matrix products, arithmetic and copies ran while one was open for 0% -> 0% of each run, Pallas kernels for 0% -> 6%
where the time goes in v1:
time: 526 us; the launch traced here: 525 us
  waiting for transfers between devices  211 us (40%)
  blocking collectives  145 us (28%)
  Pallas kernels  88.7 us (17%)
  local copies, waits for them, and re-layouts  49.6 us (9%)
  starting transfers between devices  22.1 us (4%)
  other arithmetic  7.05 us (1%)
    all_to_all x4, blocking collectives, exchange(): lax.all_to_all(blocks, 'ep', split_axis=0, concat_axis=0, tiled=True, axi...  145 us
    all_to_all x4, waiting for transfers between devices, exchange(): lax.all_to_all(blocks, 'ep', split_axis=0, concat_axis=0, tiled=True, axi...  131 us
    ppermute x3, waiting for transfers between devices, shards(): x = lax.ppermute(y, 'pp', [(moment, moment + 1), (last, last - 1)])  61.7 us
    unnamed x88, local copies, waits for them, and re-layouts  46.9 us
    pallas_call x8, Pallas kernels, hidden_units(): pl.pallas_call(hidden_kernel, out_shape=jax.ShapeDtypeStruct((rows, units...  43.2 us
    pallas_call x8, Pallas kernels, down_rows(): pl.pallas_call(down_kernel, out_shape=jax.ShapeDtypeStruct((rows, width),...  20.2 us
    ppermute x8, waiting for transfers between devices, to_sibling(): return lax.ppermute(block, 'ep', siblings)  17.8 us
    all_to_all x4, starting transfers between devices, exchange(): lax.all_to_all(blocks, 'ep', split_axis=0, concat_axis=0, tiled=True, axi...  15.5 us
  transfers between devices with their start and end apart: 15, of which 10 were waited for; matrix products, arithmetic and copies ran while one was open for 0% of the time, Pallas kernels for 6%

profile of v1, /device:TPU:0, one launch (start us, length us, event | category | flops | bytes accessed | tf_op | source)
XLA Modules:
  0.0 524.8 jit_solution(10749814156996491386)
XLA Ops:
  6.6 1.3 broadcast_select_fusion.x_ref
  7.9 1.1 dispatch.4
  9.0 38.5 %all_to_all.40 = bf16[16,40,1792]{2,1,0:T(8,128)(2,1)S(1)} all-to-all(bf16[16,40,1792]{2,1,0:T(8,128)(2,1)S(1)} %bitcast.106), channel_id=1, replica_groups={{0,2,4,6,8,10,12,14,16,18,20,22,24,26,28,30},{1,3,5,7,9,11,13,15,17,19,..., dimensions={0} | all-to-all | bytes 4587520 | tf_op jit(solution)/shard_map/all_to_all | solution.py:272
  47.5 4.4 collective-permute-done.wire_ref
  51.9 3.1 copy-done.7
  55.0 5.4 %hidden_units.9.hidden_ref = bf16[160,512]{1,0:T(8,128)(2,1)S(1)} custom-call(bf16[640,1792]{1,0:T(8,128)(2,1)S(1)} %collective-permute-done.wire_ref, bf16[320,320]{1,0:T(8,128)(2,1)S(1)} %copy-done.16, bf16[7168,512]{1,0:T(8,128)(2,1)S(1)} %bitcast.63, bf16[7168,512]{1,0:T(8,128)(2,1)S(1)} %bitcast.71), custom_call_target="tpu_custom_call" | custom-call | flops 2348810240 | bytes 16777216 | tf_op jit(solution)/shard_map/hidden_units/pallas_call | solution.py:112
  60.4 2.5 down_rows.9
  63.5 5.4 %hidden_units.8.hidden_ref = bf16[160,512]{1,0:T(8,128)(2,1)S(1)} custom-call(bf16[640,1792]{1,0:T(8,128)(2,1)S(1)} %bitcast.96, bf16[320,320]{1,0:T(8,128)(2,1)S(1)} %copy-done.16, bf16[7168,512]{1,0:T(8,128)(2,1)S(1)} %bitcast.64, bf16[7168,512]{1,0:T(8,128)(2,1)S(1)} %bitcast.72), custom_call_target="tpu_custom_call" | custom-call | flops 2348810240 | bytes 16777216 | tf_op jit(solution)/shard_map/hidden_units/pallas_call | solution.py:112
  68.9 2.5 down_rows.8.own_ref
  71.5 2.8 add_halves.4
  74.3 3.9 all-to-all-start.1
  78.3 32.8 %all-to-all-done.1 = bf16[16,40,1792]{2,1,0:T(8,128)(2,1)S(1)} async-done(((bf16[16,40,1792]{2,1,0:T(8,128)(2,1)}), bf16[16,40,1792]{2,1,0:T(8,128)(2,1)S(1)}, u32[]{:S(2)}, u32[]{:S(2)}) %all-to-all-start.1) | async-done | bytes 2293792 | tf_op jit(solution)/shard_map/all_to_all | solution.py:272
  112.1 2.7 combine.4
  114.7 3.5 collective-permute-start.2
  119.3 17.4 %collective-permute-done.2.x_ref = bf16[64,7168]{1,0:T(8,128)(2,1)S(1)} collective-permute-done((bf16[64,7168]{1,0:T(8,128)(2,1)}, bf16[64,7168]{1,0:T(8,128)(2,1)S(1)}, u32[]{:S(2)}, u32[]{:S(2)}) %collective-permute-start.2) | collective-permute-done | bytes 917536 | tf_op jit(solution)/shard_map/ppermute | solution.py:306
  138.8 34.5 %all_to_all.41 = bf16[16,40,1792]{2,1,0:T(8,128)(2,1)S(1)} all-to-all(bf16[16,40,1792]{2,1,0:T(8,128)(2,1)S(1)} %bitcast.107), channel_id=1, replica_groups={{0,2,4,6,8,10,12,14,16,18,20,22,24,26,28,30},{1,3,5,7,9,11,13,15,17,19,..., dimensions={0} | all-to-all | bytes 4587520 | tf_op jit(solution)/shard_map/all_to_all | solution.py:272
  173.3 4.4 collective-permute-done.3.wire_ref
  177.7 3.1 copy-done.1
  180.8 3.1 copy-done.9
  183.9 5.4 %hidden_units.11.hidden_ref = bf16[160,512]{1,0:T(8,128)(2,1)S(1)} custom-call(bf16[640,1792]{1,0:T(8,128)(2,1)S(1)} %collective-permute-done.3.wire_ref, bf16[320,320]{1,0:T(8,128)(2,1)S(1)} %copy-done.16, bf16[7168,512]{1,0:T(8,128)(2,1)S(1)} %bitcast.65, bf16[7168,512]{1,0:T(8,128)(2,1)S(1)} %bitcast.73), custom_call_target="tpu_custom_call" | custom-call | flops 2348810240 | bytes 16777216 | tf_op jit(solution)/shard_map/hidden_units/pallas_call | solution.py:112
  189.3 3.1 copy-done.13
  192.4 2.5 down_rows.11
  195.3 3.1 copy-done.2
  198.4 5.4 %hidden_units.10.hidden_ref = bf16[160,512]{1,0:T(8,128)(2,1)S(1)} custom-call(bf16[640,1792]{1,0:T(8,128)(2,1)S(1)} %bitcast.98, bf16[320,320]{1,0:T(8,128)(2,1)S(1)} %copy-done.16, bf16[7168,512]{1,0:T(8,128)(2,1)S(1)} %bitcast.66, bf16[7168,512]{1,0:T(8,128)(2,1)S(1)} %bitcast.74), custom_call_target="tpu_custom_call" | custom-call | flops 2348810240 | bytes 16777216 | tf_op jit(solution)/shard_map/hidden_units/pallas_call | solution.py:112
  203.9 2.5 down_rows.10.own_ref
  206.4 2.8 add_halves.5
  209.2 3.9 all-to-all-start.3
  213.2 32.9 %all-to-all-done.3 = bf16[16,40,1792]{2,1,0:T(8,128)(2,1)S(1)} async-done(((bf16[16,40,1792]{2,1,0:T(8,128)(2,1)}), bf16[16,40,1792]{2,1,0:T(8,128)(2,1)S(1)}, u32[]{:S(2)}, u32[]{:S(2)}) %all-to-all-start.3) | async-done | bytes 2293792 | tf_op jit(solution)/shard_map/all_to_all | solution.py:272
  246.1 1.2 copy-done.25
  247.3 2.7 combine.5
  250.8 1.1 dispatch.6
  251.9 36.1 %all_to_all.42 = bf16[16,40,1792]{2,1,0:T(8,128)(2,1)S(1)} all-to-all(bf16[16,40,1792]{2,1,0:T(8,128)(2,1)S(1)} %bitcast.108), channel_id=1, replica_groups={{0,2,4,6,8,10,12,14,16,18,20,22,24,26,28,30},{1,3,5,7,9,11,13,15,17,19,..., dimensions={0} | all-to-all | bytes 4587520 | tf_op jit(solution)/shard_map/all_to_all | solution.py:272
  287.9 4.4 collective-permute-done.6.wire_ref
  292.4 3.1 copy-done.3
  295.5 3.1 copy-done.10
  298.6 5.4 %hidden_units.13.hidden_ref = bf16[160,512]{1,0:T(8,128)(2,1)S(1)} custom-call(bf16[640,1792]{1,0:T(8,128)(2,1)S(1)} %collective-permute-done.6.wire_ref, bf16[320,320]{1,0:T(8,128)(2,1)S(1)} %copy-done.16, bf16[7168,512]{1,0:T(8,128)(2,1)S(1)} %bitcast.67, bf16[7168,512]{1,0:T(8,128)(2,1)S(1)} %bitcast.75), custom_call_target="tpu_custom_call" | custom-call | flops 2348810240 | bytes 16777216 | tf_op jit(solution)/shard_map/hidden_units/pallas_call | solution.py:112
  304.0 3.1 copy-done.14
  307.0 2.5 down_rows.13
  309.8 3.1 copy-done.4
  312.9 5.4 %hidden_units.12.hidden_ref = bf16[160,512]{1,0:T(8,128)(2,1)S(1)} custom-call(bf16[640,1792]{1,0:T(8,128)(2,1)S(1)} %bitcast.100, bf16[320,320]{1,0:T(8,128)(2,1)S(1)} %copy-done.16, bf16[7168,512]{1,0:T(8,128)(2,1)S(1)} %bitcast.68, bf16[7168,512]{1,0:T(8,128)(2,1)S(1)} %bitcast.76), custom_call_target="tpu_custom_call" | custom-call | flops 2348810240 | bytes 16777216 | tf_op jit(solution)/shard_map/hidden_units/pallas_call | solution.py:112
  318.3 2.5 down_rows.12.own_ref
  320.9 2.8 add_halves.6
  323.7 3.9 all-to-all-start.5
  327.7 32.6 %all-to-all-done.5 = bf16[16,40,1792]{2,1,0:T(8,128)(2,1)S(1)} async-done(((bf16[16,40,1792]{2,1,0:T(8,128)(2,1)}), bf16[16,40,1792]{2,1,0:T(8,128)(2,1)S(1)}, u32[]{:S(2)}, u32[]{:S(2)}) %all-to-all-start.5) | async-done | bytes 2293792 | tf_op jit(solution)/shard_map/all_to_all | solution.py:272
  360.4 1.2 copy-done.27
  361.5 2.7 combine.6
  364.2 1.3 collective-permute-start.8
  365.6 44.3 %collective-permute-done.8.x_ref = bf16[64,7168]{1,0:T(8,128)(2,1)S(1)} collective-permute-done((bf16[64,7168]{1,0:T(8,128)(2,1)}, bf16[64,7168]{1,0:T(8,128)(2,1)S(1)}, u32[]{:S(2)}, u32[]{:S(2)}) %collective-permute-start.8) | collective-permute-done | bytes 917536 | tf_op jit(solution)/shard_map/ppermute | solution.py:306
  409.9 1.1 dispatch.7
  411.0 36.3 %all_to_all.43 = bf16[16,40,1792]{2,1,0:T(8,128)(2,1)S(1)} all-to-all(bf16[16,40,1792]{2,1,0:T(8,128)(2,1)S(1)} %bitcast.105), channel_id=1, replica_groups={{0,2,4,6,8,10,12,14,16,18,20,22,24,26,28,30},{1,3,5,7,9,11,13,15,17,19,..., dimensions={0} | all-to-all | bytes 4587520 | tf_op jit(solution)/shard_map/all_to_all | solution.py:272
  447.3 4.4 collective-permute-done.9.wire_ref
  451.7 3.1 copy-done.5
  454.8 3.1 copy-done.11
  457.9 5.4 %hidden_units.15.hidden_ref = bf16[160,512]{1,0:T(8,128)(2,1)S(1)} custom-call(bf16[640,1792]{1,0:T(8,128)(2,1)S(1)} %collective-permute-done.9.wire_ref, bf16[320,320]{1,0:T(8,128)(2,1)S(1)} %copy-done.16, bf16[7168,512]{1,0:T(8,128)(2,1)S(1)} %bitcast.69, bf16[7168,512]{1,0:T(8,128)(2,1)S(1)} %bitcast.77), custom_call_target="tpu_custom_call" | custom-call | flops 2348810240 | bytes 16777216 | tf_op jit(solution)/shard_map/hidden_units/pallas_call | solution.py:112
  463.3 3.1 copy-done.15
  466.4 2.5 down_rows.15
  469.1 3.1 copy-done.6
  472.2 5.4 %hidden_units.14.hidden_ref = bf16[160,512]{1,0:T(8,128)(2,1)S(1)} custom-call(bf16[640,1792]{1,0:T(8,128)(2,1)S(1)} %bitcast.94, bf16[320,320]{1,0:T(8,128)(2,1)S(1)} %copy-done.16, bf16[7168,512]{1,0:T(8,128)(2,1)S(1)} %bitcast.70, bf16[7168,512]{1,0:T(8,128)(2,1)S(1)} %bitcast.78), custom_call_target="tpu_custom_call" | custom-call | flops 2348810240 | bytes 16777216 | tf_op jit(solution)/shard_map/hidden_units/pallas_call | solution.py:112
  477.7 2.5 down_rows.14.own_ref
  480.2 2.8 add_halves.7
  483.0 3.9 all-to-all-start.7
  487.0 32.9 %all-to-all-done.7 = bf16[16,40,1792]{2,1,0:T(8,128)(2,1)S(1)} async-done(((bf16[16,40,1792]{2,1,0:T(8,128)(2,1)}), bf16[16,40,1792]{2,1,0:T(8,128)(2,1)S(1)}, u32[]{:S(2)}, u32[]{:S(2)}) %all-to-all-start.7) | async-done | bytes 2293792 | tf_op jit(solution)/shard_map/all_to_all | solution.py:272
  519.9 1.8 combine.7
  521.6 3.2 select_bitcast_fusion
  (120 shorter events, 12.7 us)
Async XLA Ops:
  0.6 7.2 %copy-start.17 = (s32[640,1]{1,0:T(8,128)S(1)}, s32[640,1]{1,0:T(8,128)}, u32[]{:S(2)}) copy-start(s32[640,1]{1,0:T(8,128)} %constant.26.clone.row_ref) | copy-start | bytes 7684
  5.9 0.7 copy-start.32
  7.9 44.0 %copy-start = (bf16[1,7168,512]{2,1,0:T(8,128)(2,1)S(1)}, bf16[1,7168,512]{2,1,0:T(8,128)(2,1)}, u32[]{:S(2)}) copy-start(bf16[1,7168,512]{2,1,0:T(8,128)(2,1)} %param.19) | copy-start | bytes 22020100
  9.0 42.9 %copy-start.16 = (bf16[320,320]{1,0:T(8,128)(2,1)S(1)}, bf16[320,320]{1,0:T(8,128)(2,1)}, u32[]{:S(2)}) copy-start(bf16[320,320]{1,0:T(8,128)(2,1)} %constant.28.clone.perm_ref) | copy-start | bytes 614404
  47.5 4.4 collective-permute-start
  51.9 3.1 copy-start.7
  55.0 5.4 %copy-start.12 = (bf16[1,512,7168]{2,1,0:T(8,128)(2,1)S(1)}, bf16[1,512,7168]{2,1,0:T(8,128)(2,1)}, u32[]{:S(2)}) copy-start(bf16[1,512,7168]{2,1,0:T(8,128)(2,1)} %param.21) | copy-start | bytes 22020100
  60.4 3.1 copy-start.8
  63.0 8.5 %collective-permute-start.1 = (bf16[160,7168]{1,0:T(8,128)(2,1)S(1)}, bf16[160,7168]{1,0:T(8,128)(2,1)S(1)}, u32[]{:S(2)}, u32[]{:S(2)}) collective-permute-start(bf16[160,7168]{1,0:T(8,128)(2,1)S(1)} %down_rows.9), channel_id=1, source_target_pairs={{0,1},{1,0},{2,3},{3,2},{4,5},{5,4},{6,7},{7,6},{8,9},{9,8},{10,11... | collective-permute-start | bytes 6881288 | tf_op jit(solution)/shard_map/ppermute | solution.py:278
  68.9 2.6 copy-start.20
  74.3 3.9 copy-start.35
  74.3 3.9 copy-start.36
  74.3 36.9 %copy-start.34 = (s32[1,640]{1,0:T(1,128)S(1)}, s32[1,640]{1,0:T(1,128)}, u32[]{:S(2)}) copy-start(s32[1,640]{1,0:T(1,128)} %constant.27.clone.row_ref) | copy-start | bytes 7684
  74.3 36.8 %all-to-all-start.1 = ((bf16[16,40,1792]{2,1,0:T(8,128)(2,1)}), bf16[16,40,1792]{2,1,0:T(8,128)(2,1)S(1)}, u32[]{:S(2)}, u32[]{:S(2)}) async-start(bf16[16,40,1792]{2,1,0:T(8,128)(2,1)} %bitcast.10), calls=%async_computation.1 | async-start | bytes 4587520 | tf_op jit(solution)/shard_map/all_to_all | solution.py:272
  111.1 0.9 copy-start.33
  114.7 22.0 %collective-permute-start.2 = (bf16[64,7168]{1,0:T(8,128)(2,1)}, bf16[64,7168]{1,0:T(8,128)(2,1)S(1)}, u32[]{:S(2)}, u32[]{:S(2)}) collective-permute-start(bf16[64,7168]{1,0:T(8,128)(2,1)} %combine.4), channel_id=1, source_target_pairs={{0,32},{96,64},{1,33},{97,65},{2,34},{98,66},{3,35},{99,67},{4,36}... | collective-permute-start | bytes 2752520 | tf_op jit(solution)/shard_map/ppermute | solution.py:306
  136.7 1.0 copy-start.18
  137.7 35.6 %copy-start.24 = (bf16[64,7168]{1,0:T(8,128)(2,1)}, bf16[64,7168]{1,0:T(8,128)(2,1)S(1)}, u32[]{:S(2)}) copy-start(bf16[64,7168]{1,0:T(8,128)(2,1)S(1)} %collective-permute-done.2.x_ref) | copy-start | bytes 2752516
  173.3 4.4 collective-permute-start.3
  177.7 3.1 copy-start.1
  180.8 3.1 copy-start.9
  183.9 19.9 %slice-start = ((s8[7340032]{0:T(1024)(128)(4,1)}), s8[4194304]{0:T(1024)(128)(4,1)S(1)}, s32[]{:S(2)}) async-start(s8[7340032]{0:T(1024)(128)(4,1)} %bitcast.82), calls=%async_computation.8 | async-start | bytes 8388608
  189.3 3.1 copy-start.13
  192.4 11.4 %slice-start.1 = ((s8[7340032]{0:T(1024)(128)(4,1)}), s8[3145728]{0:T(1024)(128)(4,1)S(1)}, s32[]{:S(2)}) async-start(s8[7340032]{0:T(1024)(128)(4,1)} %bitcast.82), calls=%async_computation.9 | async-start | bytes 6291456
  194.9 11.5 %collective-permute-start.4 = (bf16[160,7168]{1,0:T(8,128)(2,1)S(1)}, bf16[160,7168]{1,0:T(8,128)(2,1)S(1)}, u32[]{:S(2)}, u32[]{:S(2)}) collective-permute-start(bf16[160,7168]{1,0:T(8,128)(2,1)S(1)} %down_rows.11), channel_id=1, source_target_pairs={{0,1},{1,0},{2,3},{3,2},{4,5},{5,4},{6,7},{7,6},{8,9},{9,8},{10,11... | collective-permute-start | bytes 6881288 | tf_op jit(solution)/shard_map/ppermute | solution.py:278
  195.3 3.1 copy-start.2
  203.8 2.6 copy-start.21
  209.2 36.9 %copy-start.31 = (s32[256,2]{1,0:T(8,128)S(1)}, s32[256,2]{1,0:T(8,128)}, u32[]{:S(2)}) copy-start(s32[256,2]{1,0:T(8,128)} %get-tuple-element.6.code_ref) | copy-start | bytes 6148
  209.2 36.8 %all-to-all-start.3 = ((bf16[16,40,1792]{2,1,0:T(8,128)(2,1)}), bf16[16,40,1792]{2,1,0:T(8,128)(2,1)S(1)}, u32[]{:S(2)}, u32[]{:S(2)}) async-start(bf16[16,40,1792]{2,1,0:T(8,128)(2,1)} %bitcast.17), calls=%async_computation.3 | async-start | bytes 4587520 | tf_op jit(solution)/shard_map/all_to_all | solution.py:272
  213.1 37.6 %copy-start.30 = (s32[256,2]{1,0:T(8,128)S(1)}, s32[256,2]{1,0:T(8,128)}, u32[]{:S(2)}) copy-start(s32[256,2]{1,0:T(8,128)} %get-tuple-element.5.code_ref) | copy-start | bytes 6148
  246.0 4.7 copy-start.19
  246.1 1.2 copy-start.25
  250.0 0.8 collective-permute-start.5
  250.8 37.2 %copy-start.26 = (bf16[64,7168]{1,0:T(8,128)(2,1)}, bf16[64,7168]{1,0:T(8,128)(2,1)S(1)}, u32[]{:S(2)}) copy-start(bf16[64,7168]{1,0:T(8,128)(2,1)S(1)} %collective-permute-done.5.x_ref) | copy-start | bytes 2752516
  287.9 4.4 collective-permute-start.6
  292.4 3.1 copy-start.3
  295.5 3.1 copy-start.10
  298.6 19.8 %slice-start.2 = ((s8[7340032]{0:T(1024)(128)(4,1)}), s8[4194304]{0:T(1024)(128)(4,1)S(1)}, s32[]{:S(2)}) async-start(s8[7340032]{0:T(1024)(128)(4,1)} %bitcast.86), calls=%async_computation.10 | async-start | bytes 8388608
  304.0 3.1 copy-start.14
  307.0 11.3 %slice-start.3 = ((s8[7340032]{0:T(1024)(128)(4,1)}), s8[3145728]{0:T(1024)(128)(4,1)S(1)}, s32[]{:S(2)}) async-start(s8[7340032]{0:T(1024)(128)(4,1)} %bitcast.86), calls=%async_computation.11 | async-start | bytes 6291456
  309.6 11.3 %collective-permute-start.7 = (bf16[160,7168]{1,0:T(8,128)(2,1)S(1)}, bf16[160,7168]{1,0:T(8,128)(2,1)S(1)}, u32[]{:S(2)}, u32[]{:S(2)}) collective-permute-start(bf16[160,7168]{1,0:T(8,128)(2,1)S(1)} %down_rows.13), channel_id=1, source_target_pairs={{0,1},{1,0},{2,3},{3,2},{4,5},{5,4},{6,7},{7,6},{8,9},{9,8},{10,11... | collective-permute-start | bytes 6881288 | tf_op jit(solution)/shard_map/ppermute | solution.py:278
  309.8 3.1 copy-start.4
  323.7 36.7 %all-to-all-start.5 = ((bf16[16,40,1792]{2,1,0:T(8,128)(2,1)}), bf16[16,40,1792]{2,1,0:T(8,128)(2,1)S(1)}, u32[]{:S(2)}, u32[]{:S(2)}) async-start(bf16[16,40,1792]{2,1,0:T(8,128)(2,1)} %bitcast.24), calls=%async_computation.5 | async-start | bytes 4587520 | tf_op jit(solution)/shard_map/all_to_all | solution.py:272
  327.6 37.9 %copy-start.28 = (s32[256,2]{1,0:T(8,128)S(1)}, s32[256,2]{1,0:T(8,128)}, u32[]{:S(2)}) copy-start(s32[256,2]{1,0:T(8,128)} %get-tuple-element.4.code_ref) | copy-start | bytes 6148
  360.4 1.2 copy-start.27
  364.2 45.6 %collective-permute-start.8 = (bf16[64,7168]{1,0:T(8,128)(2,1)}, bf16[64,7168]{1,0:T(8,128)(2,1)S(1)}, u32[]{:S(2)}, u32[]{:S(2)}) collective-permute-start(bf16[64,7168]{1,0:T(8,128)(2,1)} %combine.6), channel_id=1, source_target_pairs={{64,96},{32,0},{65,97},{33,1},{66,98},{34,2},{67,99},{35,3},{68,10... | collective-permute-start | bytes 2752520 | tf_op jit(solution)/shard_map/ppermute | solution.py:306
  409.9 37.4 %copy-start.22 = (bf16[64,7168]{1,0:T(8,128)(2,1)}, bf16[64,7168]{1,0:T(8,128)(2,1)S(1)}, u32[]{:S(2)}) copy-start(bf16[64,7168]{1,0:T(8,128)(2,1)S(1)} %collective-permute-done.8.x_ref) | copy-start | bytes 2752516
  447.3 4.4 collective-permute-start.9
  451.7 3.1 copy-start.5
  454.8 3.1 copy-start.11
  457.9 19.7 %slice-start.4 = ((s8[7340032]{0:T(1024)(128)(4,1)}), s8[4194304]{0:T(1024)(128)(4,1)S(1)}, s32[]{:S(2)}) async-start(s8[7340032]{0:T(1024)(128)(4,1)} %bitcast.90), calls=%async_computation.12 | async-start | bytes 8388608
  463.3 3.1 copy-start.15
  466.4 11.3 %slice-start.5 = ((s8[7340032]{0:T(1024)(128)(4,1)}), s8[3145728]{0:T(1024)(128)(4,1)S(1)}, s32[]{:S(2)}) async-start(s8[7340032]{0:T(1024)(128)(4,1)} %bitcast.90), calls=%async_computation.13 | async-start | bytes 6291456
  468.9 11.3 %collective-permute-start.10 = (bf16[160,7168]{1,0:T(8,128)(2,1)S(1)}, bf16[160,7168]{1,0:T(8,128)(2,1)S(1)}, u32[]{:S(2)}, u32[]{:S(2)}) collective-permute-start(bf16[160,7168]{1,0:T(8,128)(2,1)S(1)} %down_rows.15), channel_id=1, source_target_pairs={{0,1},{1,0},{2,3},{3,2},{4,5},{5,4},{6,7},{7,6},{8,9},{9,8},{10,11... | collective-permute-start | bytes 6881288 | tf_op jit(solution)/shard_map/ppermute | solution.py:278
  469.1 3.1 copy-start.6
  483.0 36.8 %copy-start.23 = (bf16[64,7168]{1,0:T(8,128)(2,1)S(1)}, bf16[64,7168]{1,0:T(8,128)(2,1)}, u32[]{:S(2)}) copy-start(bf16[64,7168]{1,0:T(8,128)(2,1)} %copy-done.22) | copy-start | bytes 2752516
  483.0 36.8 %copy-start.29 = (s32[256,2]{1,0:T(8,128)S(1)}, s32[256,2]{1,0:T(8,128)}, u32[]{:S(2)}) copy-start(s32[256,2]{1,0:T(8,128)} %get-tuple-element.4.code_ref) | copy-start | bytes 6148
  483.0 36.8 %all-to-all-start.7 = ((bf16[16,40,1792]{2,1,0:T(8,128)(2,1)}), bf16[16,40,1792]{2,1,0:T(8,128)(2,1)S(1)}, u32[]{:S(2)}, u32[]{:S(2)}) async-start(bf16[16,40,1792]{2,1,0:T(8,128)(2,1)} %bitcast.31), calls=%async_computation.7 | async-start | bytes 4587520 | tf_op jit(solution)/shard_map/all_to_all | solution.py:272
